TPU v7x, 256 devices: a whole 4x4x8 slice. The times are simulated.
256 devices in a mesh: seq: 32 (over z, y), tensor: 8 (over x, core).
Axes of the slice: x: 4, y: 4, z: 8, core: 2. Of those that a mesh axis runs over, the one named last changes fastest.
Arguments:
- linear_query: bfloat16 [8192, 4096], P('seq', 'tensor'), may hold values from -6 to 6
- linear_key: bfloat16 [8192, 4096], P('seq', 'tensor'), may hold values from -6 to 6
- linear_value: bfloat16 [8192, 4096], P('seq', 'tensor'), may hold values from -200 to 200
- output_gate: bfloat16 [8192, 4096], P('seq', 'tensor'), may hold values from -6 to 6
- log_decay: float32 [8192, 32], P('seq', 'tensor'), may hold values from -0.6 to 0
- softmax_query: bfloat16 [8192, 4096], P('seq', 'tensor'), may hold values from -4.75 to 4.75
- softmax_key: bfloat16 [8192, 4096], P('seq', 'tensor'), may hold values from -4.75 to 4.75
- document_lengths: int32 [8], replicated, may hold values from 1 to 4096, 8192 in all
Outputs:
- linear_mixed: bfloat16 [8192, 4096], P('seq', 'tensor')
- softmax_mixed: bfloat16 [8192, 4096], P('seq', 'tensor')
Inputs may be any that keep to these rules, and one draw needn't show every extreme that they name: `document_lengths`: the 8 lengths sum to 8192.
All inputs are finite; a program needn't handle non-finite values.
Results may differ from a plain program's by a relative error of at most 0.0058.
Values may be sent and summed in bfloat16 or wider, within the bound.
A program may use at most 128 MiB of HBM per device.

v0:
```python
import jax
import jax.numpy as jnp
from jax import lax
from jax.sharding import PartitionSpec as P

MIXER_COUNT = 32
HD = 128
BLOCK = 128


precise = lax.Precision.HIGHEST
floor_score = -1e30


def entering(value, axis, join, neutral):
    count, mine = (lax.axis_size(axis), lax.axis_index(axis))
    pieces = jax.tree.map(lambda part: lax.all_gather(part, axis), value)
    subtotal = jax.tree.map(
        lambda part, zero: jnp.full_like(part, 0) + jnp.asarray(zero, part.dtype), value, neutral
    )

    def step(position, subtotal):
        longer = join(subtotal, jax.tree.map(lambda part: part[position], pieces))
        return jax.tree.map(lambda new, old: jnp.where(position < mine, new, old), longer, subtotal)

    return lax.fori_loop(0, count - 1, step, subtotal)


def segments_of(positions, document_lengths):
    doc_ends = jnp.cumsum(document_lengths)
    inside = (positions[:, None] >= doc_ends[None, :]).astype(jnp.int32)
    counted = jnp.sum(inside, axis=1)
    return jnp.where(positions < 0, jnp.int32(-1), counted)


def block_step(state, inputs):
    query_blk, key_blk, value_blk, decay_blk, segment_blk, before_blk = inputs
    running = jnp.cumsum(decay_blk, axis=0)
    kept = (segment_blk == before_blk).astype(jnp.float32)
    leading = jnp.exp(running) * kept[:, None]
    carried = jnp.einsum(
        "chd,hde->che",
        query_blk.astype(jnp.float32) * leading[:, :, None],
        state,
        precision=precise,
    )
    scores = jnp.einsum("chd,jhd->hcj", query_blk, key_blk, preferred_element_type=jnp.float32)
    count = query_blk.shape[0]
    indices = jnp.arange(count, dtype=jnp.int32)
    allowed = (indices[None, :] <= indices[:, None]) & (
        segment_blk[None, :] == segment_blk[:, None]
    )
    running_t = running.T
    spread = jnp.where(allowed[None], running_t[:, :, None] - running_t[:, None, :], 0.0)
    weights = jnp.where(allowed[None], jnp.exp(spread), 0.0)
    block_weights = (scores * weights).astype(jnp.bfloat16)
    local_part = jnp.einsum(
        "hcj,jhe->che", block_weights, value_blk, preferred_element_type=jnp.float32
    )
    final_run = running[-1]
    fade = jnp.where(
        (segment_blk == segment_blk[-1])[:, None], jnp.exp(final_run[None, :] - running), 0.0
    )
    decayed = (key_blk.astype(jnp.float32) * fade[:, :, None]).astype(jnp.bfloat16)
    fresh = jnp.einsum("jhd,jhe->hde", decayed, value_blk, preferred_element_type=jnp.float32)
    state = (jnp.exp(final_run) * kept[-1])[:, None, None] * state + fresh
    return (state, carried + local_part)


def combine_states(earlier, later):
    return (earlier[0] * later[0], later[0][:, None, None] * earlier[1] + later[1])


def attend_block(
    partial_value, query_rows, query_pos, query_seg, key_heads, value_heads, key_pos, key_seg
):
    running_max, running_sum, running_out = partial_value
    scores = jnp.einsum(
        "qhd,khd->hqk", query_rows, key_heads, preferred_element_type=jnp.float32
    ) * HD ** (-0.5)
    allowed = (key_pos[None, :] <= query_pos[:, None]) & (key_seg[None, :] == query_seg[:, None])
    scores = jnp.where(allowed[None], scores, floor_score)
    new_max = jnp.maximum(running_max, jnp.max(scores, axis=2))
    raised = jnp.where(allowed[None], jnp.exp(scores - new_max[:, :, None]), 0.0)
    new_sum = jnp.sum(raised, axis=2)
    product = jnp.einsum(
        "hqk,khd->hqd", raised.astype(jnp.bfloat16), value_heads, preferred_element_type=jnp.float32
    )
    return (new_max, new_sum, product)


def on_device(
    linear_query,
    linear_key,
    linear_value,
    output_gate,
    log_decay,
    softmax_query,
    softmax_key,
    document_lengths,
):
    local_rows = linear_query.shape[0]
    local_heads = log_decay.shape[1]
    blocks = local_rows // BLOCK
    rank = lax.axis_index("seq")
    offset = rank * local_rows
    positions = offset + jnp.arange(local_rows, dtype=jnp.int32)
    segment_ids = segments_of(positions, document_lengths)
    before_ids = segments_of(positions - 1, document_lengths)
    shape = (blocks, BLOCK, local_heads, HD)
    inputs = (
        linear_query.reshape(shape),
        linear_key.reshape(shape),
        linear_value.reshape(shape),
        log_decay.reshape(blocks, BLOCK, local_heads),
        segment_ids.reshape(blocks, BLOCK),
        before_ids.reshape(blocks, BLOCK)[:, 0],
    )
    empty_state = jnp.zeros((local_heads, HD, HD), jnp.float32)
    state_end, attended = lax.scan(block_step, empty_state, inputs)
    attended = attended.reshape(local_rows, local_heads, HD)
    shard_running = jnp.cumsum(log_decay, axis=0)
    shard_kept = (segment_ids == before_ids[0]).astype(jnp.float32)
    leading = jnp.exp(shard_running) * shard_kept[:, None]
    decay_total = leading[-1]
    _, incoming = entering(
        (decay_total, state_end),
        "seq",
        combine_states,
        (jnp.ones((local_heads,), jnp.float32), empty_state),
    )
    scaled_queries = (
        linear_query.reshape(local_rows, local_heads, HD).astype(jnp.float32) * leading[:, :, None]
    )
    attended = attended + jnp.einsum("thd,hde->the", scaled_queries, incoming, precision=precise)
    power = lax.psum(jnp.sum(attended * attended, axis=(1, 2)), "tensor")
    scale = lax.rsqrt(power / (MIXER_COUNT * HD) + 1e-06)
    gated = (
        attended.reshape(local_rows, local_heads * HD)
        * scale[:, None]
        * jax.nn.sigmoid(output_gate.astype(jnp.float32))
    )
    linear_mixed = gated.astype(jnp.bfloat16)
    query_seg = segments_of(positions, document_lengths)
    query_heads = softmax_query.reshape(local_rows, local_heads, HD)
    parts = 4
    sub_rows = local_rows // parts
    latest = [
        jnp.max(positions[part_index * sub_rows : (part_index + 1) * sub_rows])
        for part_index in range(parts)
    ]
    start = jnp.int32(0)
    key_piece = lax.all_gather(softmax_key, "seq", axis=0, tiled=True)
    value_piece = lax.all_gather(linear_mixed, "seq", axis=0, tiled=True)
    count = key_piece.shape[0]
    key_heads = key_piece.reshape(count, local_heads, HD)
    value_heads = value_piece.reshape(count, local_heads, HD)
    key_pos = jnp.arange(count, dtype=jnp.int32)
    key_seg = segments_of(key_pos, document_lengths)
    running_max = jnp.full((local_heads, local_rows), floor_score, jnp.float32)
    running_sum = jnp.zeros((local_heads, local_rows), jnp.float32)
    running_out = jnp.zeros((local_heads, local_rows, HD), jnp.float32)
    max_parts = []
    sum_parts = []
    out_parts = []
    for part_index in range(parts):
        low = part_index * sub_rows
        high = low + sub_rows
        query_rows = query_heads[low:high]
        rows_pos = positions[low:high]
        rows_seg = query_seg[low:high]

        def compute(partial_value, query_rows=query_rows, rows_pos=rows_pos, rows_seg=rows_seg):
            return attend_block(
                partial_value,
                query_rows,
                rows_pos,
                rows_seg,
                key_heads,
                value_heads,
                key_pos,
                key_seg,
            )

        def untouched(partial_value):
            return partial_value

        result = lax.cond(
            start <= latest[part_index],
            compute,
            untouched,
            (running_max[:, low:high], running_sum[:, low:high], running_out[:, low:high]),
        )
        max_parts.append(result[0])
        sum_parts.append(result[1])
        out_parts.append(result[2])
    final_sum = jnp.concatenate(sum_parts, axis=1)
    final_out = jnp.concatenate(out_parts, axis=1)
    mixed = (
        (final_out / final_sum[:, :, None])
        .transpose(1, 0, 2)
        .reshape(local_rows, local_heads * HD)
        .astype(jnp.bfloat16)
    )
    return (linear_mixed, mixed)


def solution(mesh):
    return jax.shard_map(
        on_device,
        mesh=mesh,
        in_specs=(
            P("seq", "tensor"),
            P("seq", "tensor"),
            P("seq", "tensor"),
            P("seq", "tensor"),
            P("seq", "tensor"),
            P("seq", "tensor"),
            P("seq", "tensor"),
            P(),
        ),
        out_specs=(P("seq", "tensor"), P("seq", "tensor")),
        check_vma=False,
    )
```

profile of v0, /device:TPU:1, one launch (start us, length us, event | category | flops | bytes accessed | tf_op | source)
XLA Modules:
  0.0 454.8 jit_solution(11842979964522882969)
XLA Ops:
  12.2 23.9 %while.27 = (s32[]{:T(128)}, f32[4,128,128]{2,1,0:T(8,128)S(1)}, f32[2,128,4,128]{1,0,3,2:T(2,128)S(1)}, f32[2,128,4]{2,1,0:T(8,128)S(1)}, s32[2,128]{1,0:T(2,12...) while((s32[]{:T(128)}, f32[4,128,128]{2,1,0:T(8,128)S(1)}, ...), condition=%wide.region_5.6_spmd.clone, body=%wide.region_3.5_spmd.clone.sunk | while | flops 152094080 | bytes 4263464 | solution.py:120
  18.2 6.0 %dynamic_update_slice.6 = f32[2,128,4,128]{1,0,3,2:T(2,128)S(1)} dynamic-update-slice(f32[2,128,4,128]{1,0,3,2:T(2,128)S(1)} %get-tuple-element.720, f32[1,128,4,128]{1,0,3,2:T(1,128)S(1)} %copy.300, s32[]{:T(128)S(6)} %copy.305, s32[]{:T(128)} %constant.121.clone.1..sunk, s32[]{:T(128)} %constant.121.clone.1..sunk, s32[]{:T(128)} %constant.121.clone.1..sunk) | dynamic-update-slice | bytes 524292 | tf_op jit(solution)/shard_map/while/body/jit(dynamic_update_index_in_dim)/dynamic_update_slice | solution.py:120
  30.2 6.0 %dynamic_update_slice.6 = f32[2,128,4,128]{1,0,3,2:T(2,128)S(1)} dynamic-update-slice(f32[2,128,4,128]{1,0,3,2:T(2,128)S(1)} %get-tuple-element.720, f32[1,128,4,128]{1,0,3,2:T(1,128)S(1)} %copy.300, s32[]{:T(128)S(6)} %copy.305, s32[]{:T(128)} %constant.121.clone.1..sunk, s32[]{:T(128)} %constant.121.clone.1..sunk, s32[]{:T(128)} %constant.121.clone.1..sunk) | dynamic-update-slice | bytes 524292 | tf_op jit(solution)/shard_map/while/body/jit(dynamic_update_index_in_dim)/dynamic_update_slice | solution.py:120
  37.5 1.2 reduce-window.19
  40.4 37.2 %all-gather.1 = f32[32,1,4]{2,1,0:T(1,128)S(1)} all-gather(f32[1,1,4]{2,1,0:T(1,128)S(1)} %bitcast.188), channel_id=1, replica_groups=mesh['seq'=32,'tensor'=8] {'seq'}, dimensions={0}, use_global_device_ids=true | all-gather | bytes 528 | tf_op jit(solution)/shard_map/all_gather | solution.py:17
  77.5 61.4 %all-gather.10.cloned.1.call-done = f32[128,128,128]{2,1,0:T(8,128)} async-done(((f32[4,128,128]{2,1,0:T(8,128)}), f32[128,128,128]{2,1,0:T(8,128)}) %all-gather.10.cloned.1.call-update) | async-done | bytes 8388624 | tf_op jit(solution)/shard_map/all_gather | solution.py:17
  138.9 34.0 %while.28 = (s32[]{:T(128)}, f32[4,128,128]{2,1,0:T(8,128)S(1)}, s32[]{:T(128)}, f32[32,4]{1,0:T(8,128)S(1)}, f32[32,4,128,128]{3,2,1,0:T(8,128)}, /*index=5*/s32[]{:T(128)}, s32[]{:T(128)}) while((s32[]{:T(128)}, f32[4,128,128]{2,1,0:T(8,128)S(1)}, s32[]{:T(128)}, f32[32,4]{1,0:T(8,128)S(1)}, f32[32,4,128,128]{3,2,1,0:T(8,128)}, ...), condition=%wide.region_9.10_spmd.clone, body=%wide.region_8.9_spmd.clone.sunk | while | flops 262148 | bytes 786593 | solution.py:26
  140.0 1.1 fusion.96
  141.1 1.1 fusion.96
  142.2 1.1 fusion.96
  152.1 1.1 fusion.96
  155.4 1.1 fusion.96
  173.8 12.9 %psum.7 = f32[256]{0:T(256)S(1)} all-reduce(f32[256]{0:T(256)S(1)} %get-tuple-element.604), channel_id=1, replica_groups=mesh['seq'=32,'tensor'=8] {'tensor'}, use_global_device_ids=true, to_apply=%region_11.12 | all-reduce | flops 256 | bytes 2048 | tf_op jit(solution)/shard_map/psum | solution.py:136
  192.2 90.3 %all-gather.8.cloned.1.call-done = bf16[8192,512]{1,0:T(8,128)(2,1)} async-done(((bf16[256,512]{1,0:T(8,128)(2,1)}), bf16[8192,512]{1,0:T(8,128)(2,1)}) %all-gather.8.cloned.1.call-update) | async-done | bytes 8388624 | tf_op jit(solution)/shard_map/all_gather | solution.py:154
  282.4 12.5 %reshape.460 = bf16[8192,4,128]{2,1,0:T(4,128)(2,1)} reshape(bf16[8192,512]{1,0:T(8,128)(2,1)} %all-gather.8.cloned.1.call-done) | data formatting | bytes 16777216 | tf_op jit(solution)/shard_map/reshape | solution.py:157
  295.0 89.2 %all-gather.6.cloned.1.call-done = bf16[8192,512]{0,1:T(8,128)(2,1)} async-done(((bf16[256,512]{0,1:T(8,128)(2,1)}), bf16[8192,512]{0,1:T(8,128)(2,1)}) %all-gather.6.cloned.1.call-update) | async-done | bytes 8388624 | tf_op jit(solution)/shard_map/all_gather | solution.py:153
  384.3 15.7 %conditional.4 = (f32[4,64]{1,0:T(4,128)S(1)}, f32[4,64,128]{2,1,0:T(8,128)S(1)}) conditional(s32[]{:T(128)} %convert_element_type.88, () %tuple.60, (s32[8192]{0:T(1024)S(1)}, s32[64]{0:T(128)S(1)}, s32[8192]{0:T(1024)S(1)}, s32[256]{0:T(256)S(1)}, bf16[256,512]{1,0:T(8,128)(2,1)S(1)}, /*index=5*/bf16[8192,4,128]{0,2,1:T(8,128)(2,1)}, ...), branch_computations={%region_14.15_spmd, %region_15.18_spmd} | conditional | flops 1094188800 | bytes 44309520 | solution.py:188
  385.0 6.2 %fusion.77 = (f32[4,64]{1,0:T(4,128)S(1)}, f32[4,64,8192]{2,1,0:T(8,128)S(1)}) fusion(bf16[8192,4,128]{0,2,1:T(8,128)(2,1)} %get-tuple-element.527, pred[64,8192]{1,0:T(8,128)(4,1)S(1)} %compare_and_fusion, bf16[256,512]{1,0:T(8,128)(2,1)S(1)} %get-tuple-element.211), kind=kOutput, calls=%fused_computation.143 | convolution fusion | flops 543162112 | bytes 17368064 | tf_op jit(solution)/shard_map/cond/branch_1_fun/qhd,khd->hqk/dot_general | solution.py:78
  391.1 6.8 %fusion.1 = f32[4,64,128]{2,1,0:T(8,128)S(1)} fusion(bf16[8192,4,128]{2,1,0:T(4,128)(2,1)} %get-tuple-element.528, f32[4,64,8192]{2,1,0:T(8,128)S(1)} %get-tuple-element.589, f32[4,64]{1,0:T(4,128)S(1)} %broadcast_maximum_fusion, pred[64,8192]{1,0:T(8,128)(4,1)S(1)} %compare_and_fusion), kind=kOutput, calls=%fused_computation.2 | convolution fusion | flops 543162368 | bytes 17433600 | tf_op jit(solution)/shard_map/cond/branch_1_fun/hqk,khd->hqd/dot_general | solution.py:86
  397.9 2.0 fusion.4
  400.0 15.7 %conditional.5 = (f32[4,64]{1,0:T(4,128)S(1)}, f32[4,64,128]{2,1,0:T(8,128)S(1)}) conditional(s32[]{:T(128)} %convert_element_type.90, () %tuple.62, (s32[8192]{0:T(1024)S(1)}, s32[64]{0:T(128)S(1)}, s32[8192]{0:T(1024)S(1)}, s32[256]{0:T(256)S(1)}, bf16[256,512]{1,0:T(8,128)(2,1)S(1)}, /*index=5*/bf16[8192,4,128]{0,2,1:T(8,128)(2,1)}, ...), branch_computations={%region_19.20_spmd, %region_20.23_spmd} | conditional | flops 1094188800 | bytes 44309520 | solution.py:188
  400.7 6.2 %fusion.78 = (f32[4,64]{1,0:T(4,128)S(1)}, f32[4,64,8192]{2,1,0:T(8,128)S(1)}) fusion(bf16[8192,4,128]{0,2,1:T(8,128)(2,1)} %get-tuple-element.534, pred[64,8192]{1,0:T(8,128)(4,1)S(1)} %compare_and_fusion.1, bf16[256,512]{1,0:T(8,128)(2,1)S(1)} %get-tuple-element.218), kind=kOutput, calls=%fused_computation.144 | convolution fusion | flops 543162112 | bytes 17368064 | tf_op jit(solution)/shard_map/cond/branch_1_fun/qhd,khd->hqk/dot_general | solution.py:78
  406.9 6.8 %fusion.13 = f32[4,64,128]{2,1,0:T(8,128)S(1)} fusion(bf16[8192,4,128]{2,1,0:T(4,128)(2,1)} %get-tuple-element.535, f32[4,64,8192]{2,1,0:T(8,128)S(1)} %get-tuple-element.591, f32[4,64]{1,0:T(4,128)S(1)} %broadcast_maximum_fusion.1, pred[64,8192]{1,0:T(8,128)(4,1)S(1)} %compare_and_fusion.1), kind=kOutput, calls=%fused_computation.18 | convolution fusion | flops 543162368 | bytes 17433600 | tf_op jit(solution)/shard_map/cond/branch_1_fun/hqk,khd->hqd/dot_general | solution.py:86
  413.7 2.0 fusion.16
  415.7 15.7 %conditional.6 = (f32[4,64]{1,0:T(4,128)S(1)}, f32[4,64,128]{2,1,0:T(8,128)S(1)}) conditional(s32[]{:T(128)} %convert_element_type.91, () %tuple.64, (s32[8192]{0:T(1024)S(1)}, s32[64]{0:T(128)S(1)}, s32[8192]{0:T(1024)S(1)}, s32[256]{0:T(256)S(1)}, bf16[256,512]{1,0:T(8,128)(2,1)S(1)}, /*index=5*/bf16[8192,4,128]{0,2,1:T(8,128)(2,1)}, ...), branch_computations={%region_24.25_spmd, %region_25.28_spmd} | conditional | flops 1094188800 | bytes 44309520 | solution.py:188
  416.4 6.2 %fusion.79 = (f32[4,64]{1,0:T(4,128)S(1)}, f32[4,64,8192]{2,1,0:T(8,128)S(1)}) fusion(bf16[8192,4,128]{0,2,1:T(8,128)(2,1)} %get-tuple-element.541, pred[64,8192]{1,0:T(8,128)(4,1)S(1)} %compare_and_fusion.2, bf16[256,512]{1,0:T(8,128)(2,1)S(1)} %get-tuple-element.225), kind=kOutput, calls=%fused_computation.145 | convolution fusion | flops 543162112 | bytes 17368064 | tf_op jit(solution)/shard_map/cond/branch_1_fun/qhd,khd->hqk/dot_general | solution.py:78
  422.6 6.8 %fusion.25 = f32[4,64,128]{2,1,0:T(8,128)S(1)} fusion(bf16[8192,4,128]{2,1,0:T(4,128)(2,1)} %get-tuple-element.542, f32[4,64,8192]{2,1,0:T(8,128)S(1)} %get-tuple-element.593, f32[4,64]{1,0:T(4,128)S(1)} %broadcast_maximum_fusion.2, pred[64,8192]{1,0:T(8,128)(4,1)S(1)} %compare_and_fusion.2), kind=kOutput, calls=%fused_computation.34 | convolution fusion | flops 543162368 | bytes 17433600 | tf_op jit(solution)/shard_map/cond/branch_1_fun/hqk,khd->hqd/dot_general | solution.py:86
  429.4 2.0 fusion.28
  431.4 15.8 %conditional.7 = (f32[4,64]{1,0:T(4,128)S(1)}, f32[4,64,128]{2,1,0:T(8,128)S(1)}) conditional(s32[]{:T(128)} %convert_element_type.92, () %tuple.66, (s32[8192]{0:T(1024)S(1)}, s32[64]{0:T(128)S(1)}, s32[8192]{0:T(1024)S(1)}, s32[256]{0:T(256)S(1)}, bf16[256,512]{1,0:T(8,128)(2,1)S(1)}, /*index=5*/bf16[8192,4,128]{0,2,1:T(8,128)(2,1)}, ...), branch_computations={%region_29.30_spmd, %region_30.33_spmd} | conditional | flops 1094188800 | bytes 44309520 | solution.py:188
  432.2 6.2 %fusion.80 = (f32[4,64]{1,0:T(4,128)S(1)}, f32[4,64,8192]{2,1,0:T(8,128)S(1)}) fusion(bf16[8192,4,128]{0,2,1:T(8,128)(2,1)} %get-tuple-element.548, pred[64,8192]{1,0:T(8,128)(4,1)S(1)} %compare_and_fusion.3, bf16[256,512]{1,0:T(8,128)(2,1)S(1)} %get-tuple-element.232), kind=kOutput, calls=%fused_computation.146 | convolution fusion | flops 543162112 | bytes 17368064 | tf_op jit(solution)/shard_map/cond/branch_1_fun/qhd,khd->hqk/dot_general | solution.py:78
  438.4 6.8 %fusion.37 = f32[4,64,128]{2,1,0:T(8,128)S(1)} fusion(bf16[8192,4,128]{2,1,0:T(4,128)(2,1)} %get-tuple-element.549, f32[4,64,8192]{2,1,0:T(8,128)S(1)} %get-tuple-element.595, f32[4,64]{1,0:T(4,128)S(1)} %broadcast_maximum_fusion.3, pred[64,8192]{1,0:T(8,128)(4,1)S(1)} %compare_and_fusion.3), kind=kOutput, calls=%fused_computation.50 | convolution fusion | flops 543162368 | bytes 17433600 | tf_op jit(solution)/shard_map/cond/branch_1_fun/hqk,khd->hqd/dot_general | solution.py:86
  445.2 2.0 fusion.40
  (166 shorter events, 54.2 us)
Async XLA Ops:
  7.2 131.8 %all-gather.10.cloned.1.call-start = ((), (), s32[]{:S(2)}) async-start(), calls=%async_computation.2 | async-start | bytes 8650752 | tf_op jit(solution)/shard_map/all_gather | solution.py:17
  12.2 25.3 %copy-start.5 = (f32[256,4]{0,1:T(4,128)S(1)}, f32[256,4]{0,1:T(4,128)}, u32[]{:S(2)}) copy-start(f32[256,4]{0,1:T(4,128)} %param.24) | copy-start | bytes 12292
  12.2 160.8 %copy-start.1 = (bf16[256,512]{1,0:T(8,128)(2,1)S(1)}, bf16[256,512]{1,0:T(8,128)(2,1)}, u32[]{:S(2)}) copy-start(bf16[256,512]{1,0:T(8,128)(2,1)} %param.20) | copy-start | bytes 786436
  12.2 174.7 %copy-start.3 = (bf16[256,512]{1,0:T(8,128)(2,1)S(1)}, bf16[256,512]{1,0:T(8,128)(2,1)}, u32[]{:S(2)}) copy-start(bf16[256,512]{1,0:T(8,128)(2,1)} %param.23) | copy-start | bytes 786436
  36.2 0.7 copy-start
  36.2 151.7 %copy-start.4 = (bf16[256,512]{1,0:T(8,128)(2,1)S(1)}, bf16[256,512]{1,0:T(8,128)(2,1)}, u32[]{:S(2)}) copy-start(bf16[256,512]{1,0:T(8,128)(2,1)} %param.26) | copy-start | bytes 786436
  36.9 245.5 %all-gather.8.cloned.1.call-start = ((), (), s32[]{:S(2)}) async-start(), calls=%async_computation.1 | async-start | bytes 8650752 | tf_op jit(solution)/shard_map/all_gather | solution.py:154
  187.8 196.4 %all-gather.6.cloned.1.call-start = ((), (), s32[]{:S(2)}) async-start(), calls=%async_computation | async-start | bytes 8650752 | tf_op jit(solution)/shard_map/all_gather | solution.py:153
  192.2 192.1 %copy-start.2 = (bf16[256,512]{1,0:T(8,128)(2,1)S(1)}, bf16[256,512]{1,0:T(8,128)(2,1)}, u32[]{:S(2)}) copy-start(bf16[256,512]{1,0:T(8,128)(2,1)} %param.25) | copy-start | bytes 786436
Sparse Core Ops, SparseCore 0:
  37.0 101.8 all-gather.9
  187.9 94.4 all-gather.7
  285.5 98.6 all-gather.5
where the time goes:
time: 458 us; the launch traced here: 455 us
  waiting for transfers between devices  241 us (53%)
  matrix products  54.9 us (12%)
  other arithmetic  53.2 us (12%)
  blocking collectives  50 us (11%)
  local copies, waits for them, and re-layouts  37 us (8%)
  between operations  16.5 us (4%)
    all_gather x1, waiting for transfers between devices, on_device(): value_piece = lax.all_gather(linear_mixed, 'seq', axis=0, tiled=True)  90.3 us
    all_gather x1, waiting for transfers between devices, on_device(): key_piece = lax.all_gather(softmax_key, 'seq', axis=0, tiled=True)  89.2 us
    all_gather x1, waiting for transfers between devices, entering(): pieces = jax.tree.map(lambda part: lax.all_gather(part, axis), value)  61.4 us
    all_gather x1, blocking collectives, entering(): pieces = jax.tree.map(lambda part: lax.all_gather(part, axis), value)  37.2 us
    select_n x31, other arithmetic, step(): jnp.where(position < mine, new, old)  32.8 us
    dot_general x4, matrix products, attend_block(): jnp.einsum('hqk,khd->hqd', raised.astype(jnp.bfloat16), value_heads, pref...  27.2 us
    dot_general x4, matrix products, attend_block(): jnp.einsum('qhd,khd->hqk', query_rows, key_heads, preferred_element_type=...  24.7 us
    psum x1, blocking collectives, on_device(): power = lax.psum(jnp.sum(attended * attended, axis=(1, 2)), 'tensor')  12.9 us
  transfers between devices with their start and end apart: 3, of which 3 were waited for; matrix products, arithmetic and copies ran while one was open for 4% of the time, Pallas kernels for 0%

commit v1 on v0

v1 whole, which is shorter than its diff:
```python
import functools
import math

import jax
import jax.numpy as jnp
from jax import lax
from jax.experimental import pallas as pl
from jax.experimental.pallas import tpu as pltpu
from jax.sharding import PartitionSpec as P

MESH = pl.DeviceIdType.MESH
HD = 128
DOCS = 8
ROWS = 256
HEADS = 4
SEQ = 32
NZ = 8
NY = 4
WIDTH = HEADS * HD
FLOOR = -1e30
EXPONENT = math.log2(math.e) * HD**-0.5
NEAREST = (0, 1, 7, 2, 6, 3, 5, 4)
F32 = jnp.float32
BF16 = jnp.bfloat16


def mm(a, b, dims, precision=None):
    return lax.dot_general(
        a, b, (dims, ((), ())), preferred_element_type=F32, precision=precision
    )


def iota(shape, dim):
    return lax.broadcasted_iota(jnp.int32, shape, dim)


def doc_start(pos, ends):
    start = jnp.zeros_like(pos)
    for end in ends:
        start = jnp.where(pos >= end, end, start)
    return start


def kernel(
    docs, lq_h, lk_h, lv_h, gate_h, decay_h, sq_h, sk_h,
    mixed_h, out_h,
    lq, lk, lv, gate, decay, decay_pad, att,
    s_send, p1_recv, p2_send, s_in, dec_send, dec_recv, power, mix,
    keys, values, queries, scores, probs, dens, o_send, o_recv,
    load_sem, p1_ss, p1_rs, dec_ss, dec_rs, p2_ss, p2_rs, pw_ss, pw_rs,
    kz_ss, kz_rs, qz_ss, qz_rs, vz_ss, vz_rs,
    ky_ss, ky_rs, kd_ss, kd_rs, vy_ss, vy_rs, vd_ss, vd_rs, o_ss, o_rs, out_sem,
):
    s = lax.axis_index("seq")
    t = lax.axis_index("tensor")
    z, y, x, c = s // NY, s % NY, t // 2, t % 2
    sib = 2 * x + (1 - c)

    barrier = pltpu.get_barrier_semaphore()
    partners = [((s + k) % SEQ, t) for k in range(1, SEQ)]
    partners += [(((z + k) % NZ) * NY + y, sib) for k in range(NZ)]
    partners += [(s, (2 * x + 2 * k + cc) % 8) for k in range(1, 4) for cc in range(2)]
    loads = []
    for n, (src, dst) in enumerate(
        ((decay_h, decay), (lk_h, lk), (lv_h, lv), (lq_h, lq), (gate_h, gate))
    ):
        cp = pltpu.make_async_copy(src, dst, load_sem.at[n])
        cp.start()
        loads.append(cp)
    for dev in partners:
        pl.semaphore_signal(barrier, inc=1, device_id=dev, device_id_type=MESH)

    pending = []

    def remote(src, dst, ss, rs, dev):
        cp = pltpu.make_async_remote_copy(
            src_ref=src, dst_ref=dst, send_sem=ss, recv_sem=rs, device_id=dev, device_id_type=MESH
        )
        return cp

    def send(src, dst, ss, rs, dev):
        cp = remote(src, dst, ss, rs, dev)
        cp.start()
        pending.append((cp, None))

    def send_or_keep(here, src, dst, ss, rs, dev):
        cp = remote(src, dst, ss, rs, dev)

        @pl.when(jnp.logical_not(here))
        def _():
            cp.start()

        @pl.when(here)
        def _():
            pltpu.make_async_copy(src, dst, rs).start()

        pending.append((cp, here))

    def arrived(dst, rs):
        pltpu.make_async_copy(dst, dst, rs).wait()

    ends = []
    total = jnp.int32(0)
    for d in range(DOCS):
        total = total + docs[d]
        ends.append(total)
    first = s * ROWS
    pos = first + iota((ROWS, 1), 0)
    start = doc_start(pos, ends)
    last_start = doc_start(first + ROWS - 1, ends)
    kept = (start < first).astype(F32)
    in_last = pos >= last_start

    loads[0].wait()
    decay_pad[...] = jnp.zeros_like(decay_pad)
    decay_pad[:, 0:HEADS] = decay[...]
    lower = (iota((ROWS, ROWS), 1) <= iota((ROWS, ROWS), 0)).astype(F32)
    running = mm(lower, decay_pad[...], ((1,), (0,)), lax.Precision.HIGHEST)
    final = running[ROWS - 1 : ROWS, :]
    fade = jnp.where(in_last, jnp.exp(jnp.minimum(final - running, 0.0)), 0.0)
    whole = jnp.where(last_start < first, jnp.exp(final), 0.0)
    for h in range(HEADS):
        dec_send[h] = jnp.broadcast_to(whole[:, h : h + 1], (1, HD))
    loads[1].wait()
    loads[2].wait()
    for h in range(HEADS):
        cols = slice(h * HD, (h + 1) * HD)
        faded = (lk[:, cols].astype(F32) * fade[:, h : h + 1]).astype(BF16)
        s_send[h * HD : (h + 1) * HD, :] = mm(faded, lv[:, cols], ((0,), (0,))).astype(BF16)

    pl.semaphore_wait(barrier, len(partners))

    piece = 16
    order = [k for pair in zip(range(1, 17), range(31, 15, -1)) for k in pair]
    order = list(dict.fromkeys(order))
    for k in order:
        p = (s + k) % SEQ
        send(dec_send.at[p // 8], dec_recv.at[s], dec_ss.at[k], dec_rs.at[k], (p, t))
        send(
            s_send.at[pl.ds(pl.multiple_of(p * piece, piece), piece)],
            p1_recv.at[s], p1_ss.at[k], p1_rs.at[k], (p, t),
        )
    dec_recv[s] = dec_send[s // 8]
    p1_recv[s] = s_send[pl.ds(pl.multiple_of(s * piece, piece), piece), :]

    def to_heads(src, dst, ss, rs):
        for i in range(HEADS):
            for blk in range(2):
                zz = HEADS * c + i
                here = jnp.logical_and(zz == z, blk == c)
                send_or_keep(
                    here,
                    src.at[pl.ds(blk * HD, HD), pl.ds(i * HD, HD)],
                    dst(blk), ss.at[2 * i + blk], rs.at[z],
                    (zz * NY + y, 2 * x + blk),
                )

    to_heads(sk_h, lambda blk: keys.at[z, 2 * y + blk], kz_ss, kz_rs)
    to_heads(sq_h, lambda blk: queries.at[z], qz_ss, qz_rs)

    loads[3].wait()
    lead = jnp.exp(running) * kept
    running_t = running.T
    col = iota((1, ROWS), 1)
    allowed = (col <= iota((ROWS, 1), 0)) & (first + col >= start)
    for h in range(HEADS):
        cols = slice(h * HD, (h + 1) * HD)
        dots = mm(lq[:, cols], lk[:, cols], ((1,), (1,)))
        spread = jnp.where(allowed, running[:, h : h + 1] - running_t[h : h + 1, :], 0.0)
        weights = jnp.where(allowed, dots * jnp.exp(spread), 0.0).astype(BF16)
        att[:, cols] = mm(weights, lv[:, cols], ((1,), (0,)))

    for k in order:
        src = (s + SEQ - k) % SEQ
        arrived(dec_recv.at[src], dec_rs.at[k])
        arrived(p1_recv.at[src], p1_rs.at[k])
    state = jnp.zeros((piece, HD), F32)
    for r in range(SEQ):
        p2_send[r] = state.astype(BF16)
        state = dec_recv[r] * state + p1_recv[r].astype(F32)
    for k in order:
        p = (s + k) % SEQ
        send(p2_send.at[p], s_in.at[s], p2_ss.at[k], p2_rs.at[k], (p, t))
    s_in[s] = p2_send[s]

    mine = 2 * y + c
    for k in NEAREST:
        zz = (z + k) % NZ
        arrived(keys.at[zz, mine], kz_rs.at[zz])
    for k in (1, 3, 2):
        send(
            keys.at[:, mine], keys.at[:, mine], ky_ss.at[k], ky_rs.at[k],
            (z * NY + (y + k) % NY, t),
        )
    send(keys.at[:, mine], keys.at[:, mine], kd_ss.at[0], kd_rs.at[0], (s, sib))

    for k in order:
        src = (s + SEQ - k) % SEQ
        arrived(s_in.at[src], p2_rs.at[k])
    loads[4].wait()
    power_col = jnp.zeros((ROWS, 1), F32)
    for h in range(HEADS):
        cols = slice(h * HD, (h + 1) * HD)
        state_h = s_in[h * 8 : (h + 1) * 8].reshape(HD, HD)
        carried = mm(lq[:, cols], state_h, ((1,), (0,)))
        full = att[:, cols] + lead[:, h : h + 1] * carried
        att[:, cols] = full
        power_col = power_col + jnp.sum(full * full, axis=1, keepdims=True)
    diag = iota((ROWS, ROWS), 0) == iota((ROWS, ROWS), 1)
    power[t] = jnp.sum(jnp.where(diag, power_col, 0.0), axis=0, keepdims=True)
    for k in range(1, 8):
        send(power.at[t], power.at[t], pw_ss.at[k], pw_rs.at[k], (s, (t + k) % 8))
    for h in range(HEADS):
        cols = slice(h * HD, (h + 1) * HD)
        att[:, cols] = att[:, cols] * jax.nn.sigmoid(gate[:, cols].astype(F32))
    for k in range(1, 8):
        arrived(power.at[(t + 8 - k) % 8], pw_rs.at[k])
    total_row = power[0]
    for k in range(1, 8):
        total_row = total_row + power[k]
    scale_row = lax.rsqrt(total_row / (32 * HD) + 1e-06)
    scale = jnp.sum(jnp.where(diag, scale_row, 0.0), axis=1, keepdims=True)
    for h in range(HEADS):
        cols = slice(h * HD, (h + 1) * HD)
        mix[:, cols] = (att[:, cols] * scale).astype(BF16)
    to_heads(mix, lambda blk: values.at[z, 2 * y + blk], vz_ss, vz_rs)
    mixed_copy = pltpu.make_async_copy(mix, mixed_h, out_sem.at[0])
    mixed_copy.start()

    def spread_values(k):
        zz = (z + k) % NZ
        arrived(values.at[zz, mine], vz_rs.at[zz])
        for d in (1, 3, 2):
            send(
                values.at[zz, mine], values.at[zz, mine],
                vy_ss.at[k, d], vy_rs.at[zz, d], (z * NY + (y + d) % NY, t),
            )
        send(values.at[zz, mine], values.at[zz, mine], vd_ss.at[k, 0], vd_rs.at[zz, 0], (s, sib))

    def pass_values(k):
        zz = (z + k) % NZ
        for d in (1, 3, 2):
            block = 2 * ((y + NY - d) % NY) + c
            arrived(values.at[zz, block], vy_rs.at[zz, d])
            send(
                values.at[zz, block], values.at[zz, block],
                vd_ss.at[k, d], vd_rs.at[zz, d], (s, sib),
            )

    def finish_values(k):
        zz = (z + k) % NZ
        for d in range(NY):
            block = 2 * ((y + NY - d) % NY) + (1 - c)
            arrived(values.at[zz, block], vd_rs.at[zz, d])

    for k in (1, 3, 2):
        block = 2 * ((y + NY - k) % NY) + c
        arrived(keys.at[:, block], ky_rs.at[k])
        send(keys.at[:, block], keys.at[:, block], kd_ss.at[k], kd_rs.at[k], (s, sib))
    for zz in range(NZ):
        arrived(queries.at[zz], qz_rs.at[zz])
    for k in range(NY):
        block = 2 * ((y + NY - k) % NY) + (1 - c)
        arrived(keys.at[:, block], kd_rs.at[k])

    def softmax_tile(zt):
        low = max(zt - 4, 0)
        chunks = 2 * (zt - low + 1)
        q = queries[zt]
        i = zt * 1024 + y * ROWS + c * HD + iota((HD, 1), 0)
        i_start = doc_start(i, ends)

        def first_pass(g, top):
            block = keys[low + g // 2, pl.ds((g % 2) * 4, 4)].reshape(512, HD)
            dots = mm(q, block, ((1,), (1,)))
            j = low * 1024 + g * 512 + iota((1, 512), 1)
            dots = jnp.where((j <= i) & (j >= i_start), dots, FLOOR)
            scores[:, pl.ds(pl.multiple_of(g * 512, 512), 512)] = dots
            for n in range(4):
                top = jnp.maximum(top, dots[:, n * HD : (n + 1) * HD])
            return top

        top = lax.fori_loop(0, chunks, first_pass, jnp.full((HD, HD), FLOOR, F32))
        top = jnp.max(top, axis=1, keepdims=True)

        def second_pass(g, den):
            at = pl.ds(pl.multiple_of(g * 512, 512), 512)
            raised = jnp.exp2((scores[:, at] - top) * EXPONENT)
            probs[zt, :, at] = raised.astype(BF16)
            for n in range(4):
                den = den + raised[:, n * HD : (n + 1) * HD]
            return den

        den = lax.fori_loop(0, chunks, second_pass, jnp.zeros((HD, HD), F32))
        dens[zt] = jnp.broadcast_to(jnp.sum(den, axis=1, keepdims=True), (HD, HD))

    spread_values(0)
    softmax_tile(0)
    softmax_tile(1)
    spread_values(1)
    spread_values(7)
    softmax_tile(2)
    spread_values(2)
    spread_values(6)
    softmax_tile(3)
    spread_values(3)
    spread_values(5)
    spread_values(4)
    softmax_tile(4)
    pass_values(0)
    pass_values(1)
    pass_values(7)
    softmax_tile(5)
    pass_values(2)
    pass_values(6)
    softmax_tile(6)
    pass_values(3)
    pass_values(5)
    softmax_tile(7)
    pass_values(4)
    for k in NEAREST:
        finish_values(k)

    for zt in range(NZ):
        low = max(zt - 4, 0)

        def weigh(g, acc):
            at = pl.ds(pl.multiple_of(g * 1024, 1024), 1024)
            return acc + mm(
                probs[zt, :, at], values[low + g].reshape(1024, HD), ((1,), (0,))
            )

        acc = lax.fori_loop(0, zt - low + 1, weigh, jnp.zeros((HD, HD), F32))
        o_send[zt] = (acc / dens[zt]).astype(BF16)
        here = jnp.logical_and(z == zt, z // HEADS == c)
        send_or_keep(
            here, o_send.at[zt],
            o_recv.at[pl.ds(pl.multiple_of(c * HD, HD), HD), pl.ds(pl.multiple_of((z % HEADS) * HD, HD), HD)],
            o_ss.at[zt], o_rs.at[2 * (z % HEADS) + c],
            (zt * NY + y, 2 * x + z // HEADS),
        )
    for i in range(HEADS):
        for blk in range(2):
            arrived(
                o_recv.at[pl.ds(blk * HD, HD), pl.ds(i * HD, HD)], o_rs.at[2 * i + blk]
            )
    out_copy = pltpu.make_async_copy(o_recv, out_h, out_sem.at[1])
    out_copy.start()
    for cp, here in pending:
        if here is None:
            cp.wait_send()
        else:
            pl.when(jnp.logical_not(here))(cp.wait_send)
    mixed_copy.wait()
    out_copy.wait()


def on_device(lq, lk, lv, gate, decay, sq, sk, docs):
    dma = pltpu.SemaphoreType.DMA
    vmem = pltpu.VMEM
    return pl.pallas_call(
        kernel,
        out_shape=(
            jax.ShapeDtypeStruct((ROWS, WIDTH), BF16),
            jax.ShapeDtypeStruct((ROWS, WIDTH), BF16),
        ),
        in_specs=[pl.BlockSpec(memory_space=pltpu.SMEM)] + [pl.BlockSpec(memory_space=pl.ANY)] * 7,
        out_specs=(pl.BlockSpec(memory_space=pl.ANY), pl.BlockSpec(memory_space=pl.ANY)),
        scratch_shapes=[
            vmem((ROWS, WIDTH), BF16), vmem((ROWS, WIDTH), BF16),
            vmem((ROWS, WIDTH), BF16), vmem((ROWS, WIDTH), BF16),
            vmem((ROWS, HEADS), F32), vmem((ROWS, HD), F32), vmem((ROWS, WIDTH), F32),
            vmem((WIDTH, HD), BF16), vmem((SEQ, 16, HD), BF16),
            vmem((SEQ, 16, HD), BF16), vmem((SEQ, 16, HD), BF16),
            vmem((HEADS, 1, HD), F32), vmem((SEQ, 1, HD), F32),
            vmem((8, 1, ROWS), F32), vmem((ROWS, WIDTH), BF16),
            vmem((NZ, 8, HD, HD), BF16), vmem((NZ, 8, HD, HD), BF16),
            vmem((NZ, HD, HD), BF16), vmem((HD, 5 * 1024), F32),
            vmem((NZ, HD, 5 * 1024), BF16), vmem((NZ, HD, HD), F32),
            vmem((NZ, HD, HD), BF16), vmem((ROWS, WIDTH), BF16),
            dma((5,)), dma((SEQ,)), dma((SEQ,)), dma((SEQ,)), dma((SEQ,)),
            dma((SEQ,)), dma((SEQ,)), dma((8,)), dma((8,)),
            dma((8,)), dma((8,)), dma((8,)), dma((8,)), dma((8,)), dma((8,)),
            dma((4,)), dma((4,)), dma((4,)), dma((4,)),
            dma((8, 4)), dma((8, 4)), dma((8, 4)), dma((8, 4)),
            dma((8,)), dma((8,)), dma((2,)),
        ],
        compiler_params=pltpu.CompilerParams(
            collective_id=0, has_side_effects=True, vmem_limit_bytes=48 << 20
        ),
    )(docs, lq, lk, lv, gate, decay, sq, sk)


def solution(mesh):
    split = P("seq", "tensor")
    return jax.shard_map(
        on_device,
        mesh=mesh,
        in_specs=(split,) * 7 + (P(),),
        out_specs=(split, split),
        check_vma=False,
    )
```

time: 458 us -> 81.3 us (0.18)
  the two profiles are of different devices: /device:TPU:1 before, /device:TPU:224 now
where the time goes in v1:
time: 81.3 us; the launch traced here: 81 us
  Pallas kernels  72.4 us (89%)
  local copies, waits for them, and re-layouts  7.92 us (10%)
    pallas_call x1, Pallas kernels, on_device(): pl.pallas_call(kernel, out_shape=(jax.ShapeDtypeStruct((ROWS, WIDTH), BF1...  72.4 us
    unnamed x17, local copies, waits for them, and re-layouts  7.92 us

profile of v1, /device:TPU:224, one launch (start us, length us, event | category | flops | bytes accessed | tf_op | source)
XLA Modules:
  0.0 81.0 jit_solution(9384699168712015021)
XLA Ops:
  0.6 0.0 copy-start.6
  0.6 0.8 %copy.10.decay_h = f32[256,4]{1,0:T(8,128)S(1)} copy(f32[256,4]{0,1:T(4,128)} %param.12) | data formatting | bytes 8192 | tf_op args[4]
  1.5 0.0 copy-done.6
  1.5 0.0 copy-start
  1.5 0.9 %copy-done = bf16[256,512]{1,0:T(8,128)(2,1)S(1)} copy-done((bf16[256,512]{1,0:T(8,128)(2,1)S(1)}, bf16[256,512]{1,0:T(8,128)(2,1)}, u32[]{:S(2)}) %copy-start) | copy-done | bytes 262168
  2.4 0.0 copy-start.1
  2.4 0.9 %copy-done.1 = bf16[256,512]{1,0:T(8,128)(2,1)S(1)} copy-done((bf16[256,512]{1,0:T(8,128)(2,1)S(1)}, bf16[256,512]{1,0:T(8,128)(2,1)}, u32[]{:S(2)}) %copy-start.1) | copy-done | bytes 262168
  3.4 0.0 copy-start.2
  3.4 0.9 %copy-done.2 = bf16[256,512]{1,0:T(8,128)(2,1)S(1)} copy-done((bf16[256,512]{1,0:T(8,128)(2,1)S(1)}, bf16[256,512]{1,0:T(8,128)(2,1)}, u32[]{:S(2)}) %copy-start.2) | copy-done | bytes 262168
  4.3 0.0 copy-start.3
  4.3 0.9 %copy-done.3 = bf16[256,512]{1,0:T(8,128)(2,1)S(1)} copy-done((bf16[256,512]{1,0:T(8,128)(2,1)S(1)}, bf16[256,512]{1,0:T(8,128)(2,1)}, u32[]{:S(2)}) %copy-start.3) | copy-done | bytes 262168
  5.3 0.0 copy-start.4
  5.3 0.9 %copy-done.4 = bf16[256,512]{1,0:T(8,128)(2,1)S(1)} copy-done((bf16[256,512]{1,0:T(8,128)(2,1)S(1)}, bf16[256,512]{1,0:T(8,128)(2,1)}, u32[]{:S(2)}) %copy-start.4) | copy-done | bytes 262168
  6.2 0.0 copy-start.5
  6.2 0.9 %copy-done.5 = bf16[256,512]{1,0:T(8,128)(2,1)S(1)} copy-done((bf16[256,512]{1,0:T(8,128)(2,1)S(1)}, bf16[256,512]{1,0:T(8,128)(2,1)}, u32[]{:S(2)}) %copy-start.5) | copy-done | bytes 262168
  7.2 72.4 %shard_map.95 = (bf16[256,512]{1,0:T(8,128)(2,1)S(1)}, bf16[256,512]{1,0:T(8,128)(2,1)S(1)}) custom-call(s32[8]{0:T(128)S(1)} %copy-done.6, bf16[256,512]{1,0:T(8,128)(2,1)S(1)} %copy-done, bf16[256,512]{1,0:T(8,128)(2,1)S(1)} %copy-done.1, bf16[256,512]{1,0:T(8,128)(2,1)S(1)} %copy-done.2, bf16[256,512]{1,0:T(8,128)(2,1)S(1)} %copy-done.3, ...), custom_call_target="tpu_custom_call" | custom-call | tf_op jit(solution)/shard_map/pallas_call | solution.py:361
  79.6 0.7 copy.13
  80.3 0.7 copy.14
Async XLA Ops:
  0.6 0.8 %copy-start.6 = (s32[8]{0:T(128)S(1)}, s32[8]{0:T(128)}, u32[]{:S(2)}) copy-start(s32[8]{0:T(128)} %docs.1) | copy-start | bytes 100
  1.5 1.0 %copy-start = (bf16[256,512]{1,0:T(8,128)(2,1)S(1)}, bf16[256,512]{1,0:T(8,128)(2,1)}, u32[]{:S(2)}) copy-start(bf16[256,512]{1,0:T(8,128)(2,1)} %lq_h.1) | copy-start | bytes 786436
  2.4 0.9 %copy-start.1 = (bf16[256,512]{1,0:T(8,128)(2,1)S(1)}, bf16[256,512]{1,0:T(8,128)(2,1)}, u32[]{:S(2)}) copy-start(bf16[256,512]{1,0:T(8,128)(2,1)} %lk_h.1) | copy-start | bytes 786436
  3.4 0.9 %copy-start.2 = (bf16[256,512]{1,0:T(8,128)(2,1)S(1)}, bf16[256,512]{1,0:T(8,128)(2,1)}, u32[]{:S(2)}) copy-start(bf16[256,512]{1,0:T(8,128)(2,1)} %lv_h.1) | copy-start | bytes 786436
  4.3 0.9 %copy-start.3 = (bf16[256,512]{1,0:T(8,128)(2,1)S(1)}, bf16[256,512]{1,0:T(8,128)(2,1)}, u32[]{:S(2)}) copy-start(bf16[256,512]{1,0:T(8,128)(2,1)} %gate_h.1) | copy-start | bytes 786436
  5.3 0.9 %copy-start.4 = (bf16[256,512]{1,0:T(8,128)(2,1)S(1)}, bf16[256,512]{1,0:T(8,128)(2,1)}, u32[]{:S(2)}) copy-start(bf16[256,512]{1,0:T(8,128)(2,1)} %sq_h.1) | copy-start | bytes 786436
  6.2 0.9 %copy-start.5 = (bf16[256,512]{1,0:T(8,128)(2,1)S(1)}, bf16[256,512]{1,0:T(8,128)(2,1)}, u32[]{:S(2)}) copy-start(bf16[256,512]{1,0:T(8,128)(2,1)} %sk_h.1) | copy-start | bytes 786436

commit v2 on v1

--- a/solution.py
+++ b/solution.py
@@ -44,12 +44,12 @@
 def kernel(
     docs, lq_h, lk_h, lv_h, gate_h, decay_h, sq_h, sk_h,
     mixed_h, out_h,
-    lq, lk, lv, gate, decay, decay_pad, att,
-    s_send, p1_recv, p2_send, s_in, dec_send, dec_recv, power, mix,
+    lq, lk, lv, gate, decay, att,
+    s_send, p1_recv, p2_send, s_in, dec_send, dec_recv, power, mix, plain, scales, acc,
     keys, values, queries, scores, probs, dens, o_send, o_recv,
     load_sem, p1_ss, p1_rs, dec_ss, dec_rs, p2_ss, p2_rs, pw_ss, pw_rs,
     kz_ss, kz_rs, qz_ss, qz_rs, vz_ss, vz_rs,
-    ky_ss, ky_rs, kd_ss, kd_rs, vy_ss, vy_rs, vd_ss, vd_rs, o_ss, o_rs, out_sem,
+    ky_ss, ky_rs, kd_ss, kd_rs, vy_ss, vy_rs, vd_ss, vd_rs, sc_ss, sc_rs, o_ss, o_rs, out_sem,
 ):
     s = lax.axis_index("seq")
     t = lax.axis_index("tensor")
@@ -112,10 +112,15 @@
     in_last = pos >= last_start
 
     loads[0].wait()
-    decay_pad[...] = jnp.zeros_like(decay_pad)
-    decay_pad[:, 0:HEADS] = decay[...]
-    lower = (iota((ROWS, ROWS), 1) <= iota((ROWS, ROWS), 0)).astype(F32)
-    running = mm(lower, decay_pad[...], ((1,), (0,)), lax.Precision.HIGHEST)
+    lower = (iota((ROWS, ROWS), 1) <= iota((ROWS, ROWS), 0)).astype(BF16)
+    rest = decay[...]
+    running = jnp.zeros((ROWS, HEADS), F32)
+    running_t = jnp.zeros((HEADS, ROWS), F32)
+    for _ in range(3):
+        part = rest.astype(BF16)
+        rest = rest - part.astype(F32)
+        running = running + mm(lower, part, ((1,), (1,)))
+        running_t = running_t + mm(part, lower, ((1,), (1,)))
     final = running[ROWS - 1 : ROWS, :]
     fade = jnp.where(in_last, jnp.exp(jnp.minimum(final - running, 0.0)), 0.0)
     whole = jnp.where(last_start < first, jnp.exp(final), 0.0)
@@ -131,10 +136,19 @@
     pl.semaphore_wait(barrier, len(partners))
 
     piece = 16
-    order = [k for pair in zip(range(1, 17), range(31, 15, -1)) for k in pair]
-    order = list(dict.fromkeys(order))
-    for k in order:
-        p = (s + k) % SEQ
+    order = sorted(
+        range(1, SEQ),
+        key=lambda k: -min(k // NY, NZ - k // NY) - min(k % NY, NY - k % NY),
+    )
+
+    def ahead(k):
+        return (z + k // NY) % NZ * NY + (y + k % NY) % NY
+
+    def behind(k):
+        return (z + NZ - k // NY) % NZ * NY + (y + NY - k % NY) % NY
+
+    for k in order:
+        p = ahead(k)
         send(dec_send.at[p // 8], dec_recv.at[s], dec_ss.at[k], dec_rs.at[k], (p, t))
         send(
             s_send.at[pl.ds(pl.multiple_of(p * piece, piece), piece)],
@@ -144,23 +158,22 @@
     p1_recv[s] = s_send[pl.ds(pl.multiple_of(s * piece, piece), piece), :]
 
     def to_heads(src, dst, ss, rs):
-        for i in range(HEADS):
+        for n in range(HEADS):
+            i = (z + n + 1) % HEADS
             for blk in range(2):
                 zz = HEADS * c + i
                 here = jnp.logical_and(zz == z, blk == c)
                 send_or_keep(
                     here,
-                    src.at[pl.ds(blk * HD, HD), pl.ds(i * HD, HD)],
-                    dst(blk), ss.at[2 * i + blk], rs.at[z],
+                    src.at[pl.ds(blk * HD, HD), pl.ds(pl.multiple_of(i * HD, HD), HD)],
+                    dst(blk), ss.at[2 * n + blk], rs.at[z],
                     (zz * NY + y, 2 * x + blk),
                 )
 
     to_heads(sk_h, lambda blk: keys.at[z, 2 * y + blk], kz_ss, kz_rs)
-    to_heads(sq_h, lambda blk: queries.at[z], qz_ss, qz_rs)
 
     loads[3].wait()
     lead = jnp.exp(running) * kept
-    running_t = running.T
     col = iota((1, ROWS), 1)
     allowed = (col <= iota((ROWS, 1), 0)) & (first + col >= start)
     for h in range(HEADS):
@@ -171,7 +184,7 @@
         att[:, cols] = mm(weights, lv[:, cols], ((1,), (0,)))
 
     for k in order:
-        src = (s + SEQ - k) % SEQ
+        src = behind(k)
         arrived(dec_recv.at[src], dec_rs.at[k])
         arrived(p1_recv.at[src], p1_rs.at[k])
     state = jnp.zeros((piece, HD), F32)
@@ -179,9 +192,10 @@
         p2_send[r] = state.astype(BF16)
         state = dec_recv[r] * state + p1_recv[r].astype(F32)
     for k in order:
-        p = (s + k) % SEQ
+        p = ahead(k)
         send(p2_send.at[p], s_in.at[s], p2_ss.at[k], p2_rs.at[k], (p, t))
     s_in[s] = p2_send[s]
+    to_heads(sq_h, lambda blk: queries.at[z], qz_ss, qz_rs)
 
     mine = 2 * y + c
     for k in NEAREST:
@@ -195,7 +209,7 @@
     send(keys.at[:, mine], keys.at[:, mine], kd_ss.at[0], kd_rs.at[0], (s, sib))
 
     for k in order:
-        src = (s + SEQ - k) % SEQ
+        src = behind(k)
         arrived(s_in.at[src], p2_rs.at[k])
     loads[4].wait()
     power_col = jnp.zeros((ROWS, 1), F32)
@@ -212,25 +226,15 @@
         send(power.at[t], power.at[t], pw_ss.at[k], pw_rs.at[k], (s, (t + k) % 8))
     for h in range(HEADS):
         cols = slice(h * HD, (h + 1) * HD)
-        att[:, cols] = att[:, cols] * jax.nn.sigmoid(gate[:, cols].astype(F32))
-    for k in range(1, 8):
-        arrived(power.at[(t + 8 - k) % 8], pw_rs.at[k])
-    total_row = power[0]
-    for k in range(1, 8):
-        total_row = total_row + power[k]
-    scale_row = lax.rsqrt(total_row / (32 * HD) + 1e-06)
-    scale = jnp.sum(jnp.where(diag, scale_row, 0.0), axis=1, keepdims=True)
-    for h in range(HEADS):
-        cols = slice(h * HD, (h + 1) * HD)
-        mix[:, cols] = (att[:, cols] * scale).astype(BF16)
-    to_heads(mix, lambda blk: values.at[z, 2 * y + blk], vz_ss, vz_rs)
-    mixed_copy = pltpu.make_async_copy(mix, mixed_h, out_sem.at[0])
-    mixed_copy.start()
+        gated = att[:, cols] * jax.nn.sigmoid(gate[:, cols].astype(F32))
+        att[:, cols] = gated
+        plain[:, cols] = gated.astype(BF16)
+    to_heads(plain, lambda blk: values.at[z, 2 * y + blk], vz_ss, vz_rs)
 
     def spread_values(k):
         zz = (z + k) % NZ
         arrived(values.at[zz, mine], vz_rs.at[zz])
-        for d in (1, 3, 2):
+        for d in (2, 1, 3):
             send(
                 values.at[zz, mine], values.at[zz, mine],
                 vy_ss.at[k, d], vy_rs.at[zz, d], (z * NY + (y + d) % NY, t),
@@ -253,6 +257,87 @@
             block = 2 * ((y + NY - d) % NY) + (1 - c)
             arrived(values.at[zz, block], vd_rs.at[zz, d])
 
+    def weigh(k):
+        zz = (z + k) % NZ
+
+        def add(tiles):
+            part = mm(
+                probs[zz, 0:tiles].reshape(tiles * HD, 1024),
+                values[zz].reshape(1024, HD), ((1,), (0,)),
+            )
+            at = pl.ds(zz, tiles)
+            acc[at] = acc[at] + part.reshape(tiles, HD, HD)
+
+        pl.when(zz < 4)(lambda: add(5))
+        pl.when(zz >= 4)(lambda: add(4))
+
+    lane = iota((HD, HD), 1)
+
+    def first_tile(zt):
+        q = queries[zt]
+        i = zt * 1024 + y * ROWS + c * HD + iota((HD, 1), 0)
+        from_start = lane - doc_start(i, ends)
+        from_self = lane - i
+
+        def group(m, top, causal):
+            block = keys[zt - m].reshape(1024, HD)
+            for n in range(4):
+                dots = mm(q, block[n * 256 : (n + 1) * 256], ((1,), (1,)))
+                for half in range(2):
+                    base = (zt - m) * 1024 + n * 256 + half * HD
+                    allowed = from_start >= -base
+                    if causal:
+                        allowed = allowed & (from_self <= -base)
+                    at = slice(half * HD, (half + 1) * HD)
+                    part = jnp.where(allowed, dots[:, at], FLOOR)
+                    scores[zt, m, :, n * 256 + half * HD : n * 256 + (half + 1) * HD] = part
+                    top = jnp.maximum(top, part)
+            return top
+
+        top = group(0, jnp.full((HD, HD), FLOOR, F32), True)
+        top = lax.fori_loop(1, min(zt, 4) + 1, lambda m, v: group(m, v, False), top)
+        dens[zt] = jnp.broadcast_to(jnp.max(top, axis=1, keepdims=True), (HD, HD))
+
+    def second_tile(zt):
+        top = dens[zt]
+
+        def group(m, den):
+            for n in range(8):
+                at = slice(n * HD, (n + 1) * HD)
+                raised = jnp.exp2((scores[zt, m, :, at] - top) * EXPONENT)
+                den = den + raised
+                row = scales[(zt - m) * 4 + n // 2][:, (n % 2) * HD : (n % 2 + 1) * HD]
+                probs[zt - m, m, :, at] = (raised * row).astype(BF16)
+            return den
+
+        den = lax.fori_loop(0, min(zt, 4) + 1, group, jnp.zeros((HD, HD), F32))
+        dens[zt] = jnp.broadcast_to(jnp.sum(den, axis=1, keepdims=True), (HD, HD))
+
+    acc[...] = jnp.zeros_like(acc)
+    spread_values(0)
+    spread_values(1)
+    spread_values(7)
+    for k in range(1, 8):
+        arrived(power.at[(t + 8 - k) % 8], pw_rs.at[k])
+    total_row = power[0]
+    for k in range(1, 8):
+        total_row = total_row + power[k]
+    scale_row = lax.rsqrt(total_row / (32 * HD) + 1e-06)
+    scales[s] = scale_row
+    for k in order:
+        send(scales.at[s], scales.at[s], sc_ss.at[k], sc_rs.at[k], (ahead(k), t))
+    spread_values(2)
+    spread_values(6)
+    scale = jnp.sum(jnp.where(diag, scale_row, 0.0), axis=1, keepdims=True)
+    for h in range(HEADS):
+        cols = slice(h * HD, (h + 1) * HD)
+        mix[:, cols] = (att[:, cols] * scale).astype(BF16)
+    mixed_copy = pltpu.make_async_copy(mix, mixed_h, out_sem.at[0])
+    mixed_copy.start()
+    spread_values(3)
+    spread_values(5)
+    spread_values(4)
+
     for k in (1, 3, 2):
         block = 2 * ((y + NY - k) % NY) + c
         arrived(keys.at[:, block], ky_rs.at[k])
@@ -262,83 +347,48 @@
     for k in range(NY):
         block = 2 * ((y + NY - k) % NY) + (1 - c)
         arrived(keys.at[:, block], kd_rs.at[k])
-
-    def softmax_tile(zt):
-        low = max(zt - 4, 0)
-        chunks = 2 * (zt - low + 1)
-        q = queries[zt]
-        i = zt * 1024 + y * ROWS + c * HD + iota((HD, 1), 0)
-        i_start = doc_start(i, ends)
-
-        def first_pass(g, top):
-            block = keys[low + g // 2, pl.ds((g % 2) * 4, 4)].reshape(512, HD)
-            dots = mm(q, block, ((1,), (1,)))
-            j = low * 1024 + g * 512 + iota((1, 512), 1)
-            dots = jnp.where((j <= i) & (j >= i_start), dots, FLOOR)
-            scores[:, pl.ds(pl.multiple_of(g * 512, 512), 512)] = dots
-            for n in range(4):
-                top = jnp.maximum(top, dots[:, n * HD : (n + 1) * HD])
-            return top
-
-        top = lax.fori_loop(0, chunks, first_pass, jnp.full((HD, HD), FLOOR, F32))
-        top = jnp.max(top, axis=1, keepdims=True)
-
-        def second_pass(g, den):
-            at = pl.ds(pl.multiple_of(g * 512, 512), 512)
-            raised = jnp.exp2((scores[:, at] - top) * EXPONENT)
-            probs[zt, :, at] = raised.astype(BF16)
-            for n in range(4):
-                den = den + raised[:, n * HD : (n + 1) * HD]
-            return den
-
-        den = lax.fori_loop(0, chunks, second_pass, jnp.zeros((HD, HD), F32))
-        dens[zt] = jnp.broadcast_to(jnp.sum(den, axis=1, keepdims=True), (HD, HD))
-
-    spread_values(0)
-    softmax_tile(0)
-    softmax_tile(1)
-    spread_values(1)
-    spread_values(7)
-    softmax_tile(2)
-    spread_values(2)
-    spread_values(6)
-    softmax_tile(3)
-    spread_values(3)
-    spread_values(5)
-    spread_values(4)
-    softmax_tile(4)
+    for zt in range(5):
+        first_tile(zt)
     pass_values(0)
     pass_values(1)
+    first_tile(5)
+    first_tile(6)
     pass_values(7)
-    softmax_tile(5)
+    first_tile(7)
+    for k in order:
+        arrived(scales.at[behind(k)], sc_rs.at[k])
+    for zt in range(4):
+        second_tile(zt)
     pass_values(2)
+    second_tile(4)
     pass_values(6)
-    softmax_tile(6)
+    second_tile(5)
     pass_values(3)
+    second_tile(6)
     pass_values(5)
-    softmax_tile(7)
+    second_tile(7)
+    for k in NEAREST[:5]:
+        finish_values(k)
+        weigh(k)
     pass_values(4)
-    for k in NEAREST:
+    for k in NEAREST[5:]:
         finish_values(k)
-
-    for zt in range(NZ):
-        low = max(zt - 4, 0)
-
-        def weigh(g, acc):
-            at = pl.ds(pl.multiple_of(g * 1024, 1024), 1024)
-            return acc + mm(
-                probs[zt, :, at], values[low + g].reshape(1024, HD), ((1,), (0,))
-            )
-
-        acc = lax.fori_loop(0, zt - low + 1, weigh, jnp.zeros((HD, HD), F32))
-        o_send[zt] = (acc / dens[zt]).astype(BF16)
-        here = jnp.logical_and(z == zt, z // HEADS == c)
-        send_or_keep(
-            here, o_send.at[zt],
-            o_recv.at[pl.ds(pl.multiple_of(c * HD, HD), HD), pl.ds(pl.multiple_of((z % HEADS) * HD, HD), HD)],
-            o_ss.at[zt], o_rs.at[2 * (z % HEADS) + c],
-            (zt * NY + y, 2 * x + z // HEADS),
-        )
+        weigh(k)
+
+    for k in reversed(NEAREST):
+        zt = (z + k) % NZ
+        o_send[zt] = (acc[zt] / dens[zt]).astype(BF16)
+        src = o_send.at[zt]
+        dst = o_recv.at[
+            pl.ds(pl.multiple_of(c * HD, HD), HD),
+            pl.ds(pl.multiple_of((z % HEADS) * HD, HD), HD),
+        ]
+        rs = o_rs.at[2 * (z % HEADS) + c]
+        dev = (zt * NY + y, 2 * x + z // HEADS)
+        if k:
+            send(src, dst, o_ss.at[k], rs, dev)
+        else:
+            send_or_keep(z // HEADS == c, src, dst, o_ss.at[k], rs, dev)
     for i in range(HEADS):
         for blk in range(2):
             arrived(
@@ -364,31 +414,32 @@
             jax.ShapeDtypeStruct((ROWS, WIDTH), BF16),
             jax.ShapeDtypeStruct((ROWS, WIDTH), BF16),
         ),
-        in_specs=[pl.BlockSpec(memory_space=pltpu.SMEM)] + [pl.BlockSpec(memory_space=pl.ANY)] * 7,
-        out_specs=(pl.BlockSpec(memory_space=pl.ANY), pl.BlockSpec(memory_space=pl.ANY)),
+        in_specs=[pl.BlockSpec(memory_space=pltpu.SMEM)] + [pl.BlockSpec(memory_space=pltpu.HBM)] * 7,
+        out_specs=(pl.BlockSpec(memory_space=pltpu.HBM), pl.BlockSpec(memory_space=pltpu.HBM)),
         scratch_shapes=[
             vmem((ROWS, WIDTH), BF16), vmem((ROWS, WIDTH), BF16),
             vmem((ROWS, WIDTH), BF16), vmem((ROWS, WIDTH), BF16),
-            vmem((ROWS, HEADS), F32), vmem((ROWS, HD), F32), vmem((ROWS, WIDTH), F32),
+            vmem((HEADS, ROWS), F32), vmem((ROWS, WIDTH), F32),
             vmem((WIDTH, HD), BF16), vmem((SEQ, 16, HD), BF16),
             vmem((SEQ, 16, HD), BF16), vmem((SEQ, 16, HD), BF16),
             vmem((HEADS, 1, HD), F32), vmem((SEQ, 1, HD), F32),
-            vmem((8, 1, ROWS), F32), vmem((ROWS, WIDTH), BF16),
+            vmem((8, 1, ROWS), F32), vmem((ROWS, WIDTH), BF16), vmem((ROWS, WIDTH), BF16),
+            vmem((SEQ, 1, ROWS), F32), vmem((NZ + 3, HD, HD), F32),
             vmem((NZ, 8, HD, HD), BF16), vmem((NZ, 8, HD, HD), BF16),
-            vmem((NZ, HD, HD), BF16), vmem((HD, 5 * 1024), F32),
-            vmem((NZ, HD, 5 * 1024), BF16), vmem((NZ, HD, HD), F32),
+            vmem((NZ, HD, HD), BF16), vmem((NZ, 5, HD, 1024), F32),
+            vmem((NZ, 5, HD, 1024), BF16), vmem((NZ, HD, HD), F32),
             vmem((NZ, HD, HD), BF16), vmem((ROWS, WIDTH), BF16),
             dma((5,)), dma((SEQ,)), dma((SEQ,)), dma((SEQ,)), dma((SEQ,)),
             dma((SEQ,)), dma((SEQ,)), dma((8,)), dma((8,)),
             dma((8,)), dma((8,)), dma((8,)), dma((8,)), dma((8,)), dma((8,)),
             dma((4,)), dma((4,)), dma((4,)), dma((4,)),
             dma((8, 4)), dma((8, 4)), dma((8, 4)), dma((8, 4)),
-            dma((8,)), dma((8,)), dma((2,)),
+            dma((SEQ,)), dma((SEQ,)), dma((8,)), dma((8,)), dma((2,)),
         ],
         compiler_params=pltpu.CompilerParams(
-            collective_id=0, has_side_effects=True, vmem_limit_bytes=48 << 20
+            collective_id=0, has_side_effects=True, vmem_limit_bytes=(64 << 20) - (64 << 10)
         ),
-    )(docs, lq, lk, lv, gate, decay, sq, sk)
+    )(docs, lq, lk, lv, gate, decay.T, sq, sk)
 
 
 def solution(mesh):

time: 81.3 us -> 71.1 us (0.87)
  the two profiles are of different devices: /device:TPU:224 before, /device:TPU:1 now
where the time goes in v2:
time: 71.1 us; the launch traced here: 70.3 us
  Pallas kernels  67.2 us (95%)
  local copies, waits for them, and re-layouts  2.42 us (3%)
    pallas_call x1, Pallas kernels, on_device(): pl.pallas_call(kernel, out_shape=(jax.ShapeDtypeStruct((ROWS, WIDTH), BF1...  67.2 us
    unnamed x4, local copies, waits for them, and re-layouts  2.42 us

profile of v2, /device:TPU:1, one launch (start us, length us, event | category | flops | bytes accessed | tf_op | source)
XLA Modules:
  0.0 70.3 jit_solution(2378104833399940470)
XLA Ops:
  0.6 67.2 %shard_map.95 = (bf16[256,512]{1,0:T(8,128)(2,1)}, bf16[256,512]{1,0:T(8,128)(2,1)}) custom-call(s32[8]{0:T(128)} %docs.1, bf16[256,512]{1,0:T(8,128)(2,1)} %lq_h.1, bf16[256,512]{1,0:T(8,128)(2,1)} %lk_h.1, bf16[256,512]{1,0:T(8,128)(2,1)} %lv_h.1, bf16[256,512]{1,0:T(8,128)(2,1)} %gate_h.1, f32[4,256]{1,0:T(4,128)} %bitcast.1, bf16[256,512]{1,0:T(8,128)(2,1)} %sq_h.1, ...), custom_call_target="tpu_custom_call" | custom-call | tf_op jit(solution)/shard_map/pallas_call | solution.py:411
  67.8 0.0 copy-start
  67.8 1.7 %copy.12 = bf16[256,512]{1,0:T(8,128)(2,1)} copy(bf16[256,512]{1,0:T(8,128)(2,1)} %get-tuple-element.4) | data formatting | bytes 524288
  69.6 0.0 copy-done
  69.6 0.7 %copy.13 = bf16[256,512]{1,0:T(8,128)(2,1)} copy(bf16[256,512]{1,0:T(8,128)(2,1)S(1)} %copy-done) | data formatting | bytes 524288
Async XLA Ops:
  67.8 1.7 %copy-start = (bf16[256,512]{1,0:T(8,128)(2,1)S(1)}, bf16[256,512]{1,0:T(8,128)(2,1)}, u32[]{:S(2)}) copy-start(bf16[256,512]{1,0:T(8,128)(2,1)} %get-tuple-element.5) | copy-start | bytes 786436

commit v3 on v2

--- a/solution.py
+++ b/solution.py
@@ -45,7 +45,7 @@
     docs, lq_h, lk_h, lv_h, gate_h, decay_h, sq_h, sk_h,
     mixed_h, out_h,
     lq, lk, lv, gate, decay, att,
-    s_send, p1_recv, p2_send, s_in, dec_send, dec_recv, power, mix, plain, scales, acc,
+    s_send, p1_recv, p2_send, s_in, dec_send, dec_recv, power, mix, plain, scales, acc, starts,
     keys, values, queries, scores, probs, dens, o_send, o_recv,
     load_sem, p1_ss, p1_rs, dec_ss, dec_rs, p2_ss, p2_rs, pw_ss, pw_rs,
     kz_ss, kz_rs, qz_ss, qz_rs, vz_ss, vz_rs,
@@ -201,13 +201,19 @@
     for k in NEAREST:
         zz = (z + k) % NZ
         arrived(keys.at[zz, mine], kz_rs.at[zz])
-    for k in (1, 3, 2):
+    for k in (1, 3):
         send(
             keys.at[:, mine], keys.at[:, mine], ky_ss.at[k], ky_rs.at[k],
             (z * NY + (y + k) % NY, t),
         )
     send(keys.at[:, mine], keys.at[:, mine], kd_ss.at[0], kd_rs.at[0], (s, sib))
 
+    lane = iota((HD, HD), 1)
+    for zt in range(NZ):
+        row = zt * 1024 + y * ROWS + c * HD + iota((HD, 1), 0)
+        starts[zt] = lane - doc_start(row, ends)
+    dens[...] = jnp.full_like(dens, FLOOR)
+    acc[...] = jnp.zeros_like(acc)
     for k in order:
         src = behind(k)
         arrived(s_in.at[src], p2_rs.at[k])
@@ -271,35 +277,34 @@
         pl.when(zz < 4)(lambda: add(5))
         pl.when(zz >= 4)(lambda: add(4))
 
-    lane = iota((HD, HD), 1)
-
-    def first_tile(zt):
+
+    def first_part(zt, d):
+        side = (y + NY - d) % NY
         q = queries[zt]
-        i = zt * 1024 + y * ROWS + c * HD + iota((HD, 1), 0)
-        from_start = lane - doc_start(i, ends)
-        from_self = lane - i
-
-        def group(m, top, causal):
-            block = keys[zt - m].reshape(1024, HD)
-            for n in range(4):
-                dots = mm(q, block[n * 256 : (n + 1) * 256], ((1,), (1,)))
-                for half in range(2):
-                    base = (zt - m) * 1024 + n * 256 + half * HD
-                    allowed = from_start >= -base
-                    if causal:
-                        allowed = allowed & (from_self <= -base)
-                    at = slice(half * HD, (half + 1) * HD)
-                    part = jnp.where(allowed, dots[:, at], FLOOR)
-                    scores[zt, m, :, n * 256 + half * HD : n * 256 + (half + 1) * HD] = part
-                    top = jnp.maximum(top, part)
-            return top
-
-        top = group(0, jnp.full((HD, HD), FLOOR, F32), True)
-        top = lax.fori_loop(1, min(zt, 4) + 1, lambda m, v: group(m, v, False), top)
-        dens[zt] = jnp.broadcast_to(jnp.max(top, axis=1, keepdims=True), (HD, HD))
+        from_self = lane - (zt * 1024 + y * ROWS + c * HD) - iota((HD, HD), 0)
+        from_start = starts[zt]
+        top = dens[zt]
+        for m in range(min(zt, 4) + 1):
+            block = keys[zt - m, pl.ds(2 * side, 2)].reshape(256, HD)
+            dots = mm(q, block, ((1,), (1,)))
+            for half in range(2):
+                place = side * 256 + half * HD
+                base = (zt - m) * 1024 + place
+                allowed = from_start >= -base
+                if m == 0:
+                    allowed = allowed & (from_self <= -base)
+                part = jnp.where(allowed, dots[:, half * HD : (half + 1) * HD], FLOOR)
+                scores[zt, m, :, pl.ds(pl.multiple_of(place, HD), HD)] = part
+                top = jnp.maximum(top, part)
+        dens[zt] = top
+
+    def first_side(d):
+        arrived(keys.at[:, 2 * ((y + NY - d) % NY) + (1 - c)], kd_rs.at[d])
+        for zt in range(NZ):
+            first_part(zt, d)
 
     def second_tile(zt):
-        top = dens[zt]
+        top = jnp.broadcast_to(jnp.max(dens[zt], axis=1, keepdims=True), (HD, HD))
 
         def group(m, den):
             for n in range(8):
@@ -313,8 +318,16 @@
         den = lax.fori_loop(0, min(zt, 4) + 1, group, jnp.zeros((HD, HD), F32))
         dens[zt] = jnp.broadcast_to(jnp.sum(den, axis=1, keepdims=True), (HD, HD))
 
-    acc[...] = jnp.zeros_like(acc)
     spread_values(0)
+    for k in (1, 3):
+        block = 2 * ((y + NY - k) % NY) + c
+        arrived(keys.at[:, block], ky_rs.at[k])
+        half = slice(0, 4) if k == 1 else slice(4, 8)
+        send(
+            keys.at[half, block], keys.at[half, block], ky_ss.at[k - 1], ky_rs.at[k - 1],
+            (z * NY + (y + k) % NY, t),
+        )
+        send(keys.at[:, block], keys.at[:, block], kd_ss.at[k], kd_rs.at[k], (s, sib))
     spread_values(1)
     spread_values(7)
     for k in range(1, 8):
@@ -338,23 +351,19 @@
     spread_values(5)
     spread_values(4)
 
-    for k in (1, 3, 2):
-        block = 2 * ((y + NY - k) % NY) + c
-        arrived(keys.at[:, block], ky_rs.at[k])
-        send(keys.at[:, block], keys.at[:, block], kd_ss.at[k], kd_rs.at[k], (s, sib))
     for zz in range(NZ):
         arrived(queries.at[zz], qz_rs.at[zz])
-    for k in range(NY):
-        block = 2 * ((y + NY - k) % NY) + (1 - c)
-        arrived(keys.at[:, block], kd_rs.at[k])
-    for zt in range(5):
-        first_tile(zt)
+    first_side(0)
+    across = 2 * ((y + 2) % NY) + c
+    arrived(keys.at[0:4, across], ky_rs.at[0])
+    arrived(keys.at[4:8, across], ky_rs.at[2])
+    send(keys.at[:, across], keys.at[:, across], kd_ss.at[2], kd_rs.at[2], (s, sib))
+    first_side(1)
+    first_side(3)
     pass_values(0)
+    first_side(2)
     pass_values(1)
-    first_tile(5)
-    first_tile(6)
     pass_values(7)
-    first_tile(7)
     for k in order:
         arrived(scales.at[behind(k)], sc_rs.at[k])
     for zt in range(4):
@@ -405,10 +414,25 @@
     out_copy.wait()
 
 
+def settle(a, b, c, d, a_held, b_held, sems):
+    first = pltpu.make_async_copy(a, a_held, sems.at[0])
+    second = pltpu.make_async_copy(b, b_held, sems.at[1])
+    first.start()
+    second.start()
+    first.wait()
+    first = pltpu.make_async_copy(a_held, c, sems.at[2])
+    first.start()
+    second.wait()
+    second = pltpu.make_async_copy(b_held, d, sems.at[3])
+    second.start()
+    first.wait()
+    second.wait()
+
+
 def on_device(lq, lk, lv, gate, decay, sq, sk, docs):
     dma = pltpu.SemaphoreType.DMA
     vmem = pltpu.VMEM
-    return pl.pallas_call(
+    mixed, out = pl.pallas_call(
         kernel,
         out_shape=(
             jax.ShapeDtypeStruct((ROWS, WIDTH), BF16),
@@ -425,6 +449,7 @@
             vmem((HEADS, 1, HD), F32), vmem((SEQ, 1, HD), F32),
             vmem((8, 1, ROWS), F32), vmem((ROWS, WIDTH), BF16), vmem((ROWS, WIDTH), BF16),
             vmem((SEQ, 1, ROWS), F32), vmem((NZ + 3, HD, HD), F32),
+            vmem((NZ, HD, HD), jnp.int32),
             vmem((NZ, 8, HD, HD), BF16), vmem((NZ, 8, HD, HD), BF16),
             vmem((NZ, HD, HD), BF16), vmem((NZ, 5, HD, 1024), F32),
             vmem((NZ, 5, HD, 1024), BF16), vmem((NZ, HD, HD), F32),
@@ -440,6 +465,17 @@
             collective_id=0, has_side_effects=True, vmem_limit_bytes=(64 << 20) - (64 << 10)
         ),
     )(docs, lq, lk, lv, gate, decay.T, sq, sk)
+    return pl.pallas_call(
+        settle,
+        out_shape=(
+            jax.ShapeDtypeStruct((ROWS, WIDTH), BF16),
+            jax.ShapeDtypeStruct((ROWS, WIDTH), BF16),
+        ),
+        in_specs=[pl.BlockSpec(memory_space=pl.ANY)] * 2,
+        out_specs=(pl.BlockSpec(memory_space=pl.ANY), pl.BlockSpec(memory_space=pl.ANY)),
+        scratch_shapes=[vmem((ROWS, WIDTH), BF16), vmem((ROWS, WIDTH), BF16), dma((4,))],
+        compiler_params=pltpu.CompilerParams(vmem_limit_bytes=(64 << 20) - (64 << 10)),
+    )(mixed, out)
 
 
 def solution(mesh):

time: 71.1 us -> 68.1 us (0.958)
  local copies, waits for them, and re-layouts: 2.42 us -> 0 us
    unnamed x4 -> x0, local copies, waits for them, and re-layouts: 2.42 us -> none
    pallas_call x1, Pallas kernels: 67.2 us -> 65.4 us  [on_device(): pl.pallas_call(kernel, out_shape=(jax.ShapeDtypeStruct((ROWS, WIDTH), BF1...]
    pallas_call x0 -> x1, Pallas kernels: none -> 1.77 us  [on_device(): pl.pallas_call(settle, out_shape=(jax.ShapeDtypeStruct((ROWS, WIDTH), BF1...]
where the time goes in v3:
time: 68.1 us; the launch traced here: 68 us
  Pallas kernels  67.2 us (99%)
  between operations  0.8 us (1%)
    pallas_call x1, Pallas kernels, on_device(): pl.pallas_call(kernel, out_shape=(jax.ShapeDtypeStruct((ROWS, WIDTH), BF1...  65.4 us
    pallas_call x1, Pallas kernels, on_device(): pl.pallas_call(settle, out_shape=(jax.ShapeDtypeStruct((ROWS, WIDTH), BF1...  1.77 us

profile of v3, /device:TPU:1, one launch (start us, length us, event | category | flops | bytes accessed | tf_op | source)
XLA Modules:
  0.0 68.0 jit_solution(779785913652937503)
XLA Ops:
  0.6 65.4 %shard_map.95 = (bf16[256,512]{1,0:T(8,128)(2,1)}, bf16[256,512]{1,0:T(8,128)(2,1)}) custom-call(s32[8]{0:T(128)} %docs.1, bf16[256,512]{1,0:T(8,128)(2,1)} %lq_h.1, bf16[256,512]{1,0:T(8,128)(2,1)} %lk_h.1, bf16[256,512]{1,0:T(8,128)(2,1)} %lv_h.1, bf16[256,512]{1,0:T(8,128)(2,1)} %gate_h.1, f32[4,256]{1,0:T(4,128)} %bitcast.1, bf16[256,512]{1,0:T(8,128)(2,1)} %sq_h.1, ...), custom_call_target="tpu_custom_call" | custom-call | tf_op jit(solution)/shard_map/pallas_call | solution.py:435
  66.0 1.8 %shard_map.96 = (bf16[256,512]{1,0:T(8,128)(2,1)}, bf16[256,512]{1,0:T(8,128)(2,1)}) custom-call(bf16[256,512]{1,0:T(8,128)(2,1)} %get-tuple-element.4.a, bf16[256,512]{1,0:T(8,128)(2,1)} %get-tuple-element.5.b), custom_call_target="tpu_custom_call" | custom-call | tf_op jit(solution)/shard_map/pallas_call | solution.py:468

commit v4 on v3

--- a/solution.py
+++ b/solution.py
@@ -195,7 +195,6 @@
         p = ahead(k)
         send(p2_send.at[p], s_in.at[s], p2_ss.at[k], p2_rs.at[k], (p, t))
     s_in[s] = p2_send[s]
-    to_heads(sq_h, lambda blk: queries.at[z], qz_ss, qz_rs)
 
     mine = 2 * y + c
     for k in NEAREST:
@@ -208,6 +207,7 @@
         )
     send(keys.at[:, mine], keys.at[:, mine], kd_ss.at[0], kd_rs.at[0], (s, sib))
 
+    to_heads(sq_h, lambda blk: queries.at[z], qz_ss, qz_rs)
     lane = iota((HD, HD), 1)
     for zt in range(NZ):
         row = zt * 1024 + y * ROWS + c * HD + iota((HD, 1), 0)

time: 68.1 us -> 67.6 us (level)
  no operation moved by 1% of the time
where the time goes in v4:
time: 67.6 us; the launch traced here: 67.5 us
  Pallas kernels  66.7 us (99%)
  between operations  0.8 us (1%)
    pallas_call x1, Pallas kernels, on_device(): pl.pallas_call(kernel, out_shape=(jax.ShapeDtypeStruct((ROWS, WIDTH), BF1...  64.9 us
    pallas_call x1, Pallas kernels, on_device(): pl.pallas_call(settle, out_shape=(jax.ShapeDtypeStruct((ROWS, WIDTH), BF1...  1.77 us

profile of v4, /device:TPU:1, one launch (start us, length us, event | category | flops | bytes accessed | tf_op | source)
XLA Modules:
  0.0 67.5 jit_solution(4138975167301999394)
XLA Ops:
  0.6 64.9 %shard_map.95 = (bf16[256,512]{1,0:T(8,128)(2,1)}, bf16[256,512]{1,0:T(8,128)(2,1)}) custom-call(s32[8]{0:T(128)} %docs.1, bf16[256,512]{1,0:T(8,128)(2,1)} %lq_h.1, bf16[256,512]{1,0:T(8,128)(2,1)} %lk_h.1, bf16[256,512]{1,0:T(8,128)(2,1)} %lv_h.1, bf16[256,512]{1,0:T(8,128)(2,1)} %gate_h.1, f32[4,256]{1,0:T(4,128)} %bitcast.1, bf16[256,512]{1,0:T(8,128)(2,1)} %sq_h.1, ...), custom_call_target="tpu_custom_call" | custom-call | tf_op jit(solution)/shard_map/pallas_call | solution.py:435
  65.5 1.8 %shard_map.96 = (bf16[256,512]{1,0:T(8,128)(2,1)}, bf16[256,512]{1,0:T(8,128)(2,1)}) custom-call(bf16[256,512]{1,0:T(8,128)(2,1)} %get-tuple-element.4.a, bf16[256,512]{1,0:T(8,128)(2,1)} %get-tuple-element.5.b), custom_call_target="tpu_custom_call" | custom-call | tf_op jit(solution)/shard_map/pallas_call | solution.py:468
